TPU v7x, 256 devices: a whole 4x4x8 slice. The times are simulated.
256 devices in a mesh: section: 4 (over x), dp: 32 (over y, z), tensor: 2 (over core).
Axes of the slice: x: 4, y: 4, z: 8, core: 2. Of those that a mesh axis runs over, the one named last changes fastest.
Arguments:
- activations: bfloat16 [4, 16384, 12288], P('section', 'dp'), may hold values from -600 to 600
- cotangent: bfloat16 [4, 16384, 1024], P('section', 'dp', 'tensor'), may hold values from -3.59375 to 3.59375
- params: float32 [4, 12288, 1024], P('section', 'dp', 'tensor'), may hold values from -4 to 4
- first_moment: float32 [4, 12288, 1024], P('section', 'dp', 'tensor'), may hold values from -0.6 to 0.6
- second_moment: float32 [4, 12288, 1024], P('section', 'dp', 'tensor'), may hold values from 0.002 to 0.02
- step_counts: int32 [4], P('section'), may hold values from 1 to 8
Outputs:
- new_params: float32 [4, 12288, 1024], P('section', 'dp', 'tensor')
- new_first: float32 [4, 12288, 1024], P('section', 'dp', 'tensor')
- new_second: float32 [4, 12288, 1024], P('section', 'dp', 'tensor')
All inputs are finite; a program needn't handle non-finite values.
Results may differ from a plain program's by a relative error of at most 0.0003.
Values may be sent and summed in bfloat16 or wider, within the bound.
A program may use at most 128 MiB of HBM per device.

v0:
```python
import math

import jax
import jax.numpy as jnp
from jax import lax
from jax.sharding import PartitionSpec as P

beta_one = 0.9
beta_two = 0.95
learn_rate = 0.05
decay_rate = 0.1
epsilon = 1e-08
clip_scale = 0.25


def entering(part, axis, combine, identity):
    place = lax.axis_index(axis)
    gathered = lax.all_gather(part, axis)
    state = jnp.zeros_like(part) + jnp.asarray(identity, part.dtype)

    def one(hop, state):
        return combine(state, lax.dynamic_index_in_dim(gathered, hop, 0, False))

    return lax.fori_loop(0, place, one, state)


def broadcast(value, axis, root):
    mine = lax.axis_index(axis) == root
    return lax.psum(jnp.where(mine, value, jnp.zeros_like(value)), axis)


def combine_sums(earlier, later):
    return earlier + later


def body(activations, cotangent, params, first_moment, second_moment, step_counts):
    layer_input = activations[0]
    out_grads = cotangent[0]
    feature_count = layer_input.shape[1]
    unit_count = out_grads.shape[1]
    grad_shard = lax.psum_scatter(
        jnp.dot(layer_input.T, out_grads, preferred_element_type=jnp.float32),
        "dp",
        scatter_dimension=0,
        tiled=True,
    )
    local_sq = jnp.sum(grad_shard * grad_shard)
    section_sq = lax.psum(local_sq, ("dp", "tensor"))
    before = entering(section_sq, "section", combine_sums, jnp.float32(0.0))
    last_section = lax.axis_size("section") - 1
    global_sq = broadcast(before + section_sq, "section", last_section)
    threshold = clip_scale * math.sqrt(
        lax.axis_size("section") * feature_count * unit_count * lax.axis_size("tensor")
    )
    clip_factor = jnp.minimum(1.0, threshold / jnp.sqrt(global_sq))
    clipped = clip_factor * grad_shard[None]
    new_first = beta_one * first_moment + (1.0 - beta_one) * clipped
    new_second = beta_two * second_moment + (1.0 - beta_two) * clipped * clipped
    steps_now = step_counts[0].astype(jnp.float32)
    first_fix = 1.0 - jnp.power(jnp.float32(beta_one), steps_now)
    second_fix = 1.0 - jnp.power(jnp.float32(beta_two), steps_now)
    update = new_first / first_fix / (jnp.sqrt(new_second / second_fix) + epsilon)
    new_params = params * (1.0 - learn_rate * decay_rate) - learn_rate * update
    return (new_params, new_first, new_second)


def solution(mesh):
    in_specs = (
        P("section", "dp", None),
        P("section", "dp", "tensor"),
        P("section", "dp", "tensor"),
        P("section", "dp", "tensor"),
        P("section", "dp", "tensor"),
        P("section"),
    )
    out_specs = (
        P("section", "dp", "tensor"),
        P("section", "dp", "tensor"),
        P("section", "dp", "tensor"),
    )
    return jax.shard_map(body, mesh=mesh, in_specs=in_specs, out_specs=out_specs, check_vma=False)
```

profile of v0, /device:TPU:1, one launch (start us, length us, event | category | flops | bytes accessed | tf_op | source)
XLA Modules:
  0.0 452.4 jit_solution(10655344692232965272)
XLA Ops:
  7.2 0.0 copy-start
  7.2 0.0 reduce-scatter.2.cloned.1.call-start
  7.2 1.0 copy-done
  8.2 16.4 %fusion = f32[12288,512]{1,0:T(8,128)} fusion(bf16[1,512,12288]{2,1,0:T(8,128)(2,1)} %param.8, bf16[1,512,512]{2,1,0:T(8,128)(2,1)S(1)} %copy-done), kind=kOutput, calls=%fused_computation | convolution fusion | flops 6442450944 | bytes 38273024 | tf_op jit(solution)/shard_map/dot_general | solution.py:42
  24.6 0.0 copy-start.4
  24.6 0.0 copy-start.1
  24.6 0.0 copy-start.2
  24.6 0.0 copy-start.3
  24.6 0.0 reduce-scatter.2.cloned.1.call-update
  25.5 0.0 copy-done.4
  25.5 0.6 dynamic-slice
  26.1 266.1 %reduce-scatter.2.cloned.1.call-done = f32[384,512]{1,0:T(8,128)} async-done(((f32[12288,512]{1,0:T(8,128)}), f32[384,512]{1,0:T(8,128)}) %reduce-scatter.2.cloned.1.call-update) | async-done | bytes 786448 | tf_op jit(solution)/shard_map/reduce_scatter | solution.py:41
  292.2 2.0 multiply_reduce_fusion
  294.2 127.6 %psum.14 = f32[]{:T(128)} all-reduce(f32[]{:T(128)} %multiply_reduce_fusion), channel_id=1, replica_groups=mesh['section'=4,'dp'=32,'tensor'=2] {'dp','tensor'}, use_global_device_ids=true, to_apply=%region_2.0 | all-reduce | flops 1 | bytes 8 | tf_op jit(solution)/shard_map/psum | solution.py:48
  421.8 1.4 dynamic-update-slice
  423.1 8.4 %all-reduce = f32[4]{0:T(128)S(1)} all-reduce(f32[4]{0:T(128)S(1)} %dynamic-update-slice), channel_id=1, replica_groups=mesh['section'=4,'dp'=32,'tensor'=2] {'section'}, use_global_device_ids=true, to_apply=%add | all-reduce | flops 4 | bytes 32
  432.2 9.8 %psum.15 = f32[]{:T(128)} all-reduce(f32[]{:T(128)S(6)} %select_n.8), channel_id=1, replica_groups=mesh['section'=4,'dp'=32,'tensor'=2] {'section'}, use_global_device_ids=true, to_apply=%region_5.6 | all-reduce | flops 1 | bytes 8 | tf_op jit(solution)/shard_map/psum | solution.py:29
  442.6 0.0 copy-done.1
  442.6 0.0 copy-done.2
  442.6 0.0 copy-done.3
  442.7 2.9 multiply_subtract_fusion
  (2 shorter events, 0.0 us)
Async XLA Ops:
  7.2 1.0 copy-start
  7.2 285.1 %reduce-scatter.2.cloned.1.call-start = ((), (), s32[]{:S(2)}) async-start(), calls=%async_computation.1 | async-start | bytes 25952256 | tf_op jit(solution)/shard_map/reduce_scatter | solution.py:41
  24.6 0.9 copy-start.4
  24.6 418.0 %copy-start.1 = (f32[1,384,512]{2,1,0:T(8,128)S(1)}, f32[1,384,512]{2,1,0:T(8,128)}, u32[]{:S(2)}) copy-start(f32[1,384,512]{2,1,0:T(8,128)} %param.10) | copy-start | bytes 2359300
  24.6 418.0 %copy-start.2 = (f32[1,384,512]{2,1,0:T(8,128)S(1)}, f32[1,384,512]{2,1,0:T(8,128)}, u32[]{:S(2)}) copy-start(f32[1,384,512]{2,1,0:T(8,128)} %param.12) | copy-start | bytes 2359300
  24.6 418.0 %copy-start.3 = (f32[1,384,512]{2,1,0:T(8,128)S(1)}, f32[1,384,512]{2,1,0:T(8,128)}, u32[]{:S(2)}) copy-start(f32[1,384,512]{2,1,0:T(8,128)} %param.11) | copy-start | bytes 2359300
Sparse Core Ops, SparseCore 0:
  24.8 267.4 reduce-scatter.1
where the time goes:
time: 454 us; the launch traced here: 452 us
  waiting for transfers between devices  266 us (59%)
  blocking collectives  146 us (32%)
  matrix products  16.4 us (4%)
  between operations  16.3 us (4%)
  other arithmetic  4.9 us (1%)
    reduce_scatter x1, waiting for transfers between devices, body(): lax.psum_scatter(jnp.dot(layer_input.T, out_grads, preferred_element_type...  266 us
    psum x1, blocking collectives, body(): section_sq = lax.psum(local_sq, ('dp', 'tensor'))  128 us
    dot_general x1, matrix products, body(): jnp.dot(layer_input.T, out_grads, preferred_element_type=jnp.float32)  16.4 us
    psum x1, blocking collectives, broadcast(): return lax.psum(jnp.where(mine, value, jnp.zeros_like(value)), axis)  9.75 us
  transfers between devices with their start and end apart: 1, of which 1 were waited for; matrix products, arithmetic and copies ran while one was open for 0% of the time, Pallas kernels for 0%

commit v1 on v0

v1 whole, which is shorter than its diff:
```python
import functools
import math

import jax
import jax.numpy as jnp
from jax import lax
from jax.experimental import pallas as pl
from jax.experimental.pallas import tpu as pltpu
from jax.sharding import PartitionSpec as P

beta_one = 0.9
beta_two = 0.95
learn_rate = 0.05
decay_rate = 0.1
epsilon = 1e-08
clip_scale = 0.25

MESH = pl.DeviceIdType.MESH
f32 = jnp.float32

NY, NZ, DB, UN, TOK = 4, 8, 384, 512, 512
RA, RB = 304, 208
HA, HB = (160, 144), (96, 112)
TILE = 16
LEVELS = 32766.0

O_AYH = 0
O_AYF = O_AYH + NZ * RA
O_AZH = O_AYF + 2 * NZ * RA
O_AZF = O_AZH + RA
O_BZH = O_AZF + 6 * RA
O_BZF = O_BZH + NY * RB
O_BYH = O_BZF + 6 * NY * RB
O_BYF = O_BYH + RB
ROWS_ALL = O_BYF + 2 * RB
N_PIECES = 76


def piece_ayh(dz, d):
    return dz * 2 + d, O_AYH + dz * RA + d * HA[0], HA[d]


def piece_ayf(dz, d):
    return 16 + dz * 2 + d, O_AYF + (dz * 2 + d) * RA, RA


def piece_azh(d):
    return 32 + d, O_AZH + d * HA[0], HA[d]


def piece_azf(j, d):
    return 34 + (j - 1) * 2 + d, O_AZF + ((j - 1) * 2 + d) * RA, RA


def piece_bzh(dy, d):
    return 40 + dy * 2 + d, O_BZH + dy * RB + d * HB[0], HB[d]


def piece_bzf(dy, j, d):
    return 48 + dy * 6 + (j - 1) * 2 + d, O_BZF + (dy * 6 + (j - 1) * 2 + d) * RB, RB


def piece_byh(d):
    return 72 + d, O_BYH + d * HB[0], HB[d]


def piece_byf(d):
    return 74 + d, O_BYF + d * RB, RB


SCHEDULE = [20, 276, 284, 21, 268, 19, 260, 307, 92, 341, 44, 315, 349, 93, 43, 299, 333, 91, 370, 374, 45, 291, 382, 22, 378, 366, 18, 362, 325, 17, 94, 46, 100, 367, 377, 90, 42, 375, 369, 89, 131, 165, 41, 361, 383, 23, 354, 16, 358, 400, 194, 198, 95, 47, 353, 359, 88, 40, 193, 199, 472, 424, 480, 224]


def firsts(schedule):
    seen, marks = [], []
    for code in schedule:
        block = code % 32
        marks.append(0 if block in seen else len(seen) + 1)
        if block not in seen:
            seen.append(block)
    return seen, marks


BLOCK_ORDER, FIRST_USE = firsts(SCHEDULE)


def pick(table, index):
    value = jnp.int32(table[0])
    for place in range(1, len(table)):
        value = jnp.where(index == place, jnp.int32(table[place]), value)
    return value


PEERS_C = [(0, 0, 0, 1)]
PEERS_XY = [(i, j, 0, 0) for i in range(4) for j in range(4) if i or j]
PEERS_Z = [(0, 0, i, 0) for i in range(1, 8)]


def kernel(act_ref, cot_ref, grad_ref, sq_ref, act, cot_t, total, final, send, recv, send_scale, recv_scale,
           sq_vec, sq_c, sq_xy, sq_z, sq_out, act_sem, send_sem, recv_sem, send_scale_sem, recv_scale_sem,
           norm_send_sem, norm_recv_sem):
    section = lax.axis_index("section")
    dp = lax.axis_index("dp")
    core = lax.axis_index("tensor")
    y, z = lax.div(dp, NZ), lax.rem(dp, NZ)

    def peer(dx, dy, dz, dc):
        return (
            lax.rem(section + dx, 4),
            lax.rem(y + dy, NY) * NZ + lax.rem(z + dz, NZ),
            lax.rem(core + dc, 2),
        )

    def block_columns(dy, dz):
        block = lax.rem(y + dy, NY) * NZ + lax.rem(z + dz, NZ)
        return pl.ds(pl.multiple_of(block * DB, DB), DB)

    barrier = pltpu.get_barrier_semaphore()
    peers = PEERS_C + PEERS_XY + PEERS_Z
    for offset in peers:
        pl.semaphore_signal(barrier, inc=1, device_id=peer(*offset), device_id_type=MESH)

    def act_copy(order, offset):
        columns = block_columns(offset // NZ, offset % NZ)
        return pltpu.make_async_copy(act_ref.at[0, :, columns], act.at[:, columns], act_sem.at[order])

    @pl.loop(0, NY * NZ)
    def _(order):
        act_copy(order, pick(BLOCK_ORDER, order)).start()

    cot_t[...] = cot_ref[0].T
    pl.semaphore_wait(barrier, len(peers))

    def rows_of(offset, count):
        return pl.ds(pl.multiple_of(offset, TILE), count)

    def copies(piece, to):
        number, offset, count = piece
        rows = rows_of(offset, count)
        data = pltpu.make_async_remote_copy(
            src_ref=send.at[rows], dst_ref=recv.at[rows], send_sem=send_sem.at[number], recv_sem=recv_sem.at[number],
            device_id=to, device_id_type=MESH)
        scale = pltpu.make_async_remote_copy(
            src_ref=send_scale.at[number], dst_ref=recv_scale.at[number], send_sem=send_scale_sem.at[number],
            recv_sem=recv_scale_sem.at[number], device_id=to, device_id_type=MESH)
        return data, scale

    nowhere = peer(0, 0, 0, 1)

    def step(in_a, dy, dz, arrivals, departures):
        start, count = (0, RA) if in_a else (RA, RB)
        total[pl.ds(0, count)] = jnp.dot(
            cot_t[pl.ds(start, count)], act[:, block_columns(dy, dz)], preferred_element_type=f32)
        scales = []
        for piece, _ in arrivals:
            for copy in copies(piece, nowhere):
                copy.wait_recv()
            scales.append(recv_scale[piece[0]])
        top = jnp.zeros((8, DB), f32)
        for row in range(0, count, TILE):
            value = total[pl.ds(row, TILE)]
            for (piece, first), scale in zip(arrivals, scales):
                if first <= row < first + piece[2]:
                    code = recv[rows_of(piece[1] + (row - first), TILE)]
                    value = value + code.astype(jnp.int32).astype(f32) * scale
            if departures:
                if arrivals:
                    total[pl.ds(row, TILE)] = value
                size = jnp.abs(value)
                top = jnp.maximum(top, jnp.maximum(size[:8], size[8:]))
            else:
                final[pl.ds(start + row, TILE)] = value
                square = value * value
                top = top + (square[:8] + square[8:])
        if not departures:
            sq_vec[0 if in_a else 1] = top
            return
        top = jnp.maximum(jnp.max(top, axis=0, keepdims=True), 1e-30)
        inverse = LEVELS / top
        for piece, first, to in departures:
            number, offset, size = piece
            send_scale[number] = top * (1.0 / LEVELS)
            for row in range(0, size, TILE):
                code = jnp.round(total[pl.ds(first + row, TILE)] * inverse)
                send[rows_of(offset + row, TILE)] = code.astype(jnp.int32).astype(jnp.int16)
            for copy in copies(piece, to):
                copy.start()

    y_peer = (peer(0, 1, 0, 0), peer(0, NY - 1, 0, 0))
    z_peer = (peer(0, 0, 1, 0), peer(0, 0, NZ - 1, 0))

    def z_toward(d):
        return peer(0, 0, 1 + (NZ - 2) * d, 0)

    @pl.loop(0, len(SCHEDULE))
    def _(index):
        code = pick(SCHEDULE, index)
        first_use = pick(FIRST_USE, index)
        kind, offset = lax.div(code, 32), lax.rem(code, 32)
        dy, dz = lax.div(offset, NZ), lax.rem(offset, NZ)

        @pl.when(first_use > 0)
        def _():
            act_copy(first_use - 1, offset).wait()

        def when(value):
            return pl.when(kind == value)

        @when(0)
        def _():
            step(True, dy, dz, [], [
                (piece_ayh(dz, 0), 0, y_peer[0]), (piece_ayh(dz, 1), HA[0], y_peer[1])])

        for d in (0, 1):
            @when(1 + d)
            def _(d=d):
                step(True, dy, dz, [(piece_ayh(dz, d), d * HA[0])], [(piece_ayf(dz, d), 0, y_peer[d])])

        def summed_over_y():
            return [(piece_ayf(dz, 0), 0), (piece_ayf(dz, 1), 0)]

        @when(3)
        def _():
            step(True, dy, dz, summed_over_y(), [
                (piece_azh(0), 0, z_peer[0]), (piece_azh(1), HA[0], z_peer[1])])

        for d in (0, 1):
            @when(4 + d)
            def _(d=d):
                step(True, dy, dz, summed_over_y() + [(piece_azh(d), d * HA[0])], [(piece_azf(3, d), 0, z_peer[d])])

        toward = (dz > NZ // 2).astype(jnp.int32)
        hops = jnp.where(dz > NZ // 2, NZ - dz, dz)

        @when(6)
        def _():
            step(True, dy, dz, summed_over_y() + [(piece_azf(hops + 1, toward), 0)],
                 [(piece_azf(hops, toward), 0, z_toward(toward))])

        @when(7)
        def _():
            step(True, dy, dz, summed_over_y() + [(piece_azf(1, 0), 0), (piece_azf(1, 1), 0)], [])

        @when(8)
        def _():
            step(False, dy, dz, [], [
                (piece_bzh(dy, 0), 0, z_peer[0]), (piece_bzh(dy, 1), HB[0], z_peer[1])])

        for d in (0, 1):
            @when(9 + d)
            def _(d=d):
                step(False, dy, dz, [(piece_bzh(dy, d), d * HB[0])], [(piece_bzf(dy, 3, d), 0, z_peer[d])])

        @when(11)
        def _():
            step(False, dy, dz, [(piece_bzf(dy, hops + 1, toward), 0)],
                 [(piece_bzf(dy, hops, toward), 0, z_toward(toward))])

        def summed_over_z():
            return [(piece_bzf(dy, 1, 0), 0), (piece_bzf(dy, 1, 1), 0)]

        @when(12)
        def _():
            step(False, dy, dz, summed_over_z(), [
                (piece_byh(0), 0, y_peer[0]), (piece_byh(1), HB[0], y_peer[1])])

        for d in (0, 1):
            @when(13 + d)
            def _(d=d):
                step(False, dy, dz, summed_over_z() + [(piece_byh(d), d * HB[0])], [(piece_byf(d), 0, y_peer[d])])

        @when(15)
        def _():
            step(False, dy, dz, summed_over_z() + [(piece_byf(0), 0), (piece_byf(1), 0)], [])

    lanes = jnp.sum(sq_vec[0] + sq_vec[1], axis=0, keepdims=True)
    value = lanes[:, :128] + lanes[:, 128:256] + lanes[:, 256:]
    place = 0
    waiting = []
    for stage, (offsets, slots) in enumerate(((PEERS_C, sq_c), (PEERS_XY, sq_xy), (PEERS_Z, sq_z))):
        sq_out[stage] = value
        exchange = []
        for slot, offset in enumerate(offsets):
            copy = pltpu.make_async_remote_copy(
                src_ref=sq_out.at[stage], dst_ref=slots.at[slot], send_sem=norm_send_sem.at[place],
                recv_sem=norm_recv_sem.at[place], device_id=peer(*offset), device_id_type=MESH)
            copy.start()
            exchange.append(copy)
            place += 1
        if stage == 1:
            grad_ref[...] = final[...].T
        for copy in exchange:
            copy.wait_recv()
        for slot in range(len(offsets)):
            value = value + slots[slot]
        waiting += exchange
    sq_ref[...] = jnp.broadcast_to(jnp.sum(value, axis=1, keepdims=True), (8, 128))

    for copy in waiting:
        copy.wait_send()

    def sent(count, piece):
        @pl.loop(0, count)
        def _(index):
            for copy in copies(piece(index), nowhere):
                copy.wait_send()

    for d in (0, 1):
        sent(NZ, lambda i, d=d: piece_ayh(i, d))
        sent(NZ, lambda i, d=d: piece_ayf(i, d))
        sent(1, lambda i, d=d: piece_azh(d))
        sent(3, lambda i, d=d: piece_azf(i + 1, d))
        sent(NY, lambda i, d=d: piece_bzh(i, d))
        for dy in range(NY):
            sent(3, lambda i, d=d, dy=dy: piece_bzf(dy, i + 1, d))
        sent(1, lambda i, d=d: piece_byh(d))
        sent(1, lambda i, d=d: piece_byf(d))


def reduced_gradient(activations, cotangent):
    dma = pltpu.SemaphoreType.DMA
    return pl.pallas_call(
        kernel,
        out_shape=(jax.ShapeDtypeStruct((DB, UN), f32), jax.ShapeDtypeStruct((8, 128), f32)),
        in_specs=[pl.BlockSpec(memory_space=pl.ANY), pl.BlockSpec(memory_space=pltpu.VMEM)],
        out_specs=[pl.BlockSpec(memory_space=pltpu.VMEM)] * 2,
        scratch_shapes=[
            pltpu.VMEM((TOK, NY * NZ * DB), jnp.bfloat16),
            pltpu.VMEM((UN, TOK), jnp.bfloat16),
            pltpu.VMEM((RA, DB), f32),
            pltpu.VMEM((UN, DB), f32),
            pltpu.VMEM((ROWS_ALL, DB), jnp.int16),
            pltpu.VMEM((ROWS_ALL, DB), jnp.int16),
            pltpu.VMEM((N_PIECES, 1, DB), f32),
            pltpu.VMEM((N_PIECES, 1, DB), f32),
            pltpu.VMEM((2, 8, DB), f32),
            pltpu.VMEM((1, 1, 128), f32),
            pltpu.VMEM((15, 1, 128), f32),
            pltpu.VMEM((7, 1, 128), f32),
            pltpu.VMEM((3, 1, 128), f32),
            dma((NY * NZ,)),
            dma((N_PIECES,)),
            dma((N_PIECES,)),
            dma((N_PIECES,)),
            dma((N_PIECES,)),
            dma((23,)),
            dma((23,)),
        ],
        compiler_params=pltpu.CompilerParams(collective_id=0, has_side_effects=True, vmem_limit_bytes=56 << 20),
    )(activations, cotangent)


def body(activations, cotangent, params, first_moment, second_moment, step_counts):
    feature_count = activations.shape[2]
    unit_count = cotangent.shape[2]
    grad_shard, squares = reduced_gradient(activations, cotangent)
    global_sq = squares[0, 0]
    threshold = clip_scale * math.sqrt(
        lax.axis_size("section") * feature_count * unit_count * lax.axis_size("tensor")
    )
    clip_factor = jnp.minimum(1.0, threshold / jnp.sqrt(global_sq))
    clipped = clip_factor * grad_shard[None]
    new_first = beta_one * first_moment + (1.0 - beta_one) * clipped
    new_second = beta_two * second_moment + (1.0 - beta_two) * clipped * clipped
    steps_now = step_counts[0].astype(jnp.float32)
    first_fix = 1.0 - jnp.power(jnp.float32(beta_one), steps_now)
    second_fix = 1.0 - jnp.power(jnp.float32(beta_two), steps_now)
    update = new_first / first_fix / (jnp.sqrt(new_second / second_fix) + epsilon)
    new_params = params * (1.0 - learn_rate * decay_rate) - learn_rate * update
    return (new_params, new_first, new_second)


def solution(mesh):
    in_specs = (
        P("section", "dp", None),
        P("section", "dp", "tensor"),
        P("section", "dp", "tensor"),
        P("section", "dp", "tensor"),
        P("section", "dp", "tensor"),
        P("section"),
    )
    out_specs = (
        P("section", "dp", "tensor"),
        P("section", "dp", "tensor"),
        P("section", "dp", "tensor"),
    )
    return jax.shard_map(body, mesh=mesh, in_specs=in_specs, out_specs=out_specs, check_vma=False)
```

time: 454 us -> 101 us (0.22)
  waiting for transfers between devices: 266 us -> 0 us
  blocking collectives: 146 us -> 0 us
  Pallas kernels: 0 us -> 94.6 us
  matrix products: 16.4 us -> 0 us
  between operations: 16.3 us -> 2.26 us
    reduce_scatter x1 -> x0, waiting for transfers between devices: 266 us -> none  [body(): lax.psum_scatter(jnp.dot(layer_input.T, out_grads, preferred_element_type...]
    psum x2 -> x0, blocking collectives: 137 us -> none  [the longest x1 128 us: body(): section_sq = lax.psum(local_sq, ('dp', 'tensor'))]
    pallas_call x0 -> x1, Pallas kernels: none -> 94.6 us  [reduced_gradient(): pl.pallas_call(kernel, out_shape=(jax.ShapeDtypeStruct((DB, UN), f32), ja...]
    dot_general x1 -> x0, matrix products: 16.4 us -> none  [body(): jnp.dot(layer_input.T, out_grads, preferred_element_type=jnp.float32)]
    unnamed x1 -> x0, blocking collectives: 8.39 us -> none
  transfers between devices with their start and end apart: 1 -> 0, of which waited for: 1 -> 0; matrix products, arithmetic and copies ran while one was open for 0% -> 0% of each run, Pallas kernels for 0% -> 0%
where the time goes in v1:
time: 101 us
  Pallas kernels  94.6 us (94%)
  other arithmetic  2.93 us (3%)
  between operations  2.26 us (2%)
  local copies, waits for them, and re-layouts  1.21 us (1%)
    pallas_call x1, Pallas kernels, reduced_gradient(): pl.pallas_call(kernel, out_shape=(jax.ShapeDtypeStruct((DB, UN), f32), ja...  94.6 us
    sub x1, other arithmetic, body(): new_params = params * (1.0 - learn_rate * decay_rate) - learn_rate * update  2.93 us

profile of v1, /device:TPU:1, one launch (start us, length us, event | category | flops | bytes accessed | tf_op | source)
XLA Modules:
  0.0 101.0 jit_solution(13779017521431375544)
XLA Ops:
  0.6 0.0 copy-start.1
  0.6 0.0 copy-start.2
  0.7 0.0 copy-start
  1.5 94.6 %shard_map.85 = (f32[384,512]{1,0:T(8,128)}, f32[8,128]{1,0:T(8,128)}) custom-call(bf16[1,512,12288]{2,1,0:T(8,128)(2,1)} %act_ref.1, bf16[1,512,512]{2,1,0:T(8,128)(2,1)} %cot_ref.1), custom_call_target="tpu_custom_call" | custom-call | tf_op jit(solution)/shard_map/pallas_call | solution.py:322
  96.1 1.2 %slice.3 = f32[1,1]{1,0:T(1,128)} slice(f32[8,128]{1,0:T(8,128)} %get-tuple-element.5), slice={[0:1], [0:1]} | slice | bytes 8 | tf_op jit(solution)/shard_map/slice | solution.py:357
  98.0 0.0 copy-done.1
  98.0 0.0 copy-done.2
  98.0 0.0 copy-done
  98.0 2.9 %multiply_subtract_fusion = (f32[1,384,512]{2,1,0:T(8,128)}, f32[1,384,512]{2,1,0:T(8,128)}, f32[1,384,512]{2,1,0:T(8,128)}) fusion(f32[1,384,512]{2,1,0:T(8,128)S(1)} %copy-done, f32[]{:T(128)} %bitcast.4, f32[]{:T(128)} %bitcast.2, f32[384,512]{1,0:T(8,128)} %get-tuple-element.6, f32[]{:T(128)} %bitcast, f32[1,384,512]{2,1,0:T(8,128)S(1)} %copy-done.1, ...), kind=kLoop, calls=%fused_computation.4 | loop fusion | flops 2949120 | bytes 5505036 | tf_op jit(solution)/shard_map/sub | solution.py:369
Async XLA Ops:
  0.6 97.4 %copy-start.1 = (f32[1,384,512]{2,1,0:T(8,128)S(1)}, f32[1,384,512]{2,1,0:T(8,128)}, u32[]{:S(2)}) copy-start(f32[1,384,512]{2,1,0:T(8,128)} %param.10) | copy-start | bytes 2359300
  0.6 97.4 %copy-start.2 = (f32[1,384,512]{2,1,0:T(8,128)S(1)}, f32[1,384,512]{2,1,0:T(8,128)}, u32[]{:S(2)}) copy-start(f32[1,384,512]{2,1,0:T(8,128)} %param.9) | copy-start | bytes 2359300
  0.7 97.4 %copy-start = (f32[1,384,512]{2,1,0:T(8,128)S(1)}, f32[1,384,512]{2,1,0:T(8,128)}, u32[]{:S(2)}) copy-start(f32[1,384,512]{2,1,0:T(8,128)} %param.8) | copy-start | bytes 2359300

commit v2 on v1

--- a/solution.py
+++ b/solution.py
@@ -68,7 +68,7 @@
     return 74 + d, O_BYF + d * RB, RB
 
 
-SCHEDULE = [20, 276, 284, 21, 268, 19, 260, 307, 92, 341, 44, 315, 349, 93, 43, 299, 333, 91, 370, 374, 45, 291, 382, 22, 378, 366, 18, 362, 325, 17, 94, 46, 100, 367, 377, 90, 42, 375, 369, 89, 131, 165, 41, 361, 383, 23, 354, 16, 358, 400, 194, 198, 95, 47, 353, 359, 88, 40, 193, 199, 472, 424, 480, 224]
+SCHEDULE = [20, 268, 19, 276, 260, 18, 284, 22, 299, 333, 21, 291, 341, 44, 92, 307, 349, 23, 315, 93, 366, 45, 362, 374, 43, 100, 91, 354, 378, 325, 17, 367, 94, 46, 370, 165, 42, 131, 90, 47, 375, 377, 95, 369, 382, 16, 89, 198, 194, 358, 41, 383, 361, 400, 353, 88, 40, 199, 193, 424, 359, 472, 224, 480]
 
 
 def firsts(schedule):
@@ -85,10 +85,16 @@
 
 
 def pick(table, index):
-    value = jnp.int32(table[0])
-    for place in range(1, len(table)):
-        value = jnp.where(index == place, jnp.int32(table[place]), value)
-    return value
+    values = [jnp.int32(entry) for entry in table]
+    step = 1
+    while len(values) > 1:
+        odd = lax.rem(lax.div(index, step), 2) == 1
+        values = [jnp.where(odd, b, a) for a, b in zip(values[::2], values[1::2], strict=True)]
+        step *= 2
+    return values[0]
+
+
+EARLY = 2
 
 
 PEERS_C = [(0, 0, 0, 1)]
@@ -96,9 +102,9 @@
 PEERS_Z = [(0, 0, i, 0) for i in range(1, 8)]
 
 
-def kernel(act_ref, cot_ref, grad_ref, sq_ref, act, cot_t, total, final, send, recv, send_scale, recv_scale,
+def kernel(act_ref, cot_hbm, grad_ref, clip_ref, act, cot_t, total, final, send, recv, send_scale, recv_scale,
            sq_vec, sq_c, sq_xy, sq_z, sq_out, act_sem, send_sem, recv_sem, send_scale_sem, recv_scale_sem,
-           norm_send_sem, norm_recv_sem):
+           norm_send_sem, norm_recv_sem, cot_ref, cot_sem):
     section = lax.axis_index("section")
     dp = lax.axis_index("dp")
     core = lax.axis_index("tensor")
@@ -120,6 +126,9 @@
     for offset in peers:
         pl.semaphore_signal(barrier, inc=1, device_id=peer(*offset), device_id_type=MESH)
 
+    cot_copy = pltpu.make_async_copy(cot_hbm.at[0], cot_ref, cot_sem)
+    cot_copy.start()
+
     def act_copy(order, offset):
         columns = block_columns(offset // NZ, offset % NZ)
         return pltpu.make_async_copy(act_ref.at[0, :, columns], act.at[:, columns], act_sem.at[order])
@@ -128,9 +137,8 @@
     def _(order):
         act_copy(order, pick(BLOCK_ORDER, order)).start()
 
-    cot_t[...] = cot_ref[0].T
-    pl.semaphore_wait(barrier, len(peers))
-
+    cot_copy.wait()
+    cot_t[...] = cot_ref[...].T
     def rows_of(offset, count):
         return pl.ds(pl.multiple_of(offset, TILE), count)
 
@@ -147,7 +155,12 @@
 
     nowhere = peer(0, 0, 0, 1)
 
-    def step(in_a, dy, dz, arrivals, departures):
+    def send_off(departures):
+        for piece, _, to in departures:
+            for copy in copies(piece, to):
+                copy.start()
+
+    def step(index, in_a, dy, dz, arrivals, departures):
         start, count = (0, RA) if in_a else (RA, RB)
         total[pl.ds(0, count)] = jnp.dot(
             cot_t[pl.ds(start, count)], act[:, block_columns(dy, dz)], preferred_element_type=f32)
@@ -183,19 +196,33 @@
             for row in range(0, size, TILE):
                 code = jnp.round(total[pl.ds(first + row, TILE)] * inverse)
                 send[rows_of(offset + row, TILE)] = code.astype(jnp.int32).astype(jnp.int16)
-            for copy in copies(piece, to):
-                copy.start()
+        if arrivals:
+            send_off(departures)
+        else:
+            pl.when(index >= EARLY)(lambda: send_off(departures))
 
     y_peer = (peer(0, 1, 0, 0), peer(0, NY - 1, 0, 0))
     z_peer = (peer(0, 0, 1, 0), peer(0, 0, NZ - 1, 0))
 
+    def first_of_a(dz):
+        return [(piece_ayh(dz, 0), 0, y_peer[0]), (piece_ayh(dz, 1), HA[0], y_peer[1])]
+
+    def first_of_b(dy):
+        return [(piece_bzh(dy, 0), 0, z_peer[0]), (piece_bzh(dy, 1), HB[0], z_peer[1])]
+
     def z_toward(d):
         return peer(0, 0, 1 + (NZ - 2) * d, 0)
 
     @pl.loop(0, len(SCHEDULE))
     def _(index):
-        code = pick(SCHEDULE, index)
-        first_use = pick(FIRST_USE, index)
+        @pl.when(index == EARLY)
+        def _():
+            pl.semaphore_wait(barrier, len(peers))
+            for early in SCHEDULE[:EARLY]:
+                send_off(first_of_a(early % NZ) if early < 32 else first_of_b(early // NZ % NY))
+
+        entry = pick([code * 64 + mark for code, mark in zip(SCHEDULE, FIRST_USE)], index)
+        code, first_use = lax.div(entry, 64), lax.rem(entry, 64)
         kind, offset = lax.div(code, 32), lax.rem(code, 32)
         dy, dz = lax.div(offset, NZ), lax.rem(offset, NZ)
 
@@ -203,57 +230,57 @@
         def _():
             act_copy(first_use - 1, offset).wait()
 
+        kinds = {}
+
         def when(value):
-            return pl.when(kind == value)
+            return functools.partial(kinds.__setitem__, value)
 
         @when(0)
         def _():
-            step(True, dy, dz, [], [
-                (piece_ayh(dz, 0), 0, y_peer[0]), (piece_ayh(dz, 1), HA[0], y_peer[1])])
+            step(index, True, dy, dz, [], first_of_a(dz))
 
         for d in (0, 1):
             @when(1 + d)
             def _(d=d):
-                step(True, dy, dz, [(piece_ayh(dz, d), d * HA[0])], [(piece_ayf(dz, d), 0, y_peer[d])])
+                step(index, True, dy, dz, [(piece_ayh(dz, d), d * HA[0])], [(piece_ayf(dz, d), 0, y_peer[d])])
 
         def summed_over_y():
             return [(piece_ayf(dz, 0), 0), (piece_ayf(dz, 1), 0)]
 
         @when(3)
         def _():
-            step(True, dy, dz, summed_over_y(), [
+            step(index, True, dy, dz, summed_over_y(), [
                 (piece_azh(0), 0, z_peer[0]), (piece_azh(1), HA[0], z_peer[1])])
 
         for d in (0, 1):
             @when(4 + d)
             def _(d=d):
-                step(True, dy, dz, summed_over_y() + [(piece_azh(d), d * HA[0])], [(piece_azf(3, d), 0, z_peer[d])])
+                step(index, True, dy, dz, summed_over_y() + [(piece_azh(d), d * HA[0])], [(piece_azf(3, d), 0, z_peer[d])])
 
         toward = (dz > NZ // 2).astype(jnp.int32)
         hops = jnp.where(dz > NZ // 2, NZ - dz, dz)
 
         @when(6)
         def _():
-            step(True, dy, dz, summed_over_y() + [(piece_azf(hops + 1, toward), 0)],
+            step(index, True, dy, dz, summed_over_y() + [(piece_azf(hops + 1, toward), 0)],
                  [(piece_azf(hops, toward), 0, z_toward(toward))])
 
         @when(7)
         def _():
-            step(True, dy, dz, summed_over_y() + [(piece_azf(1, 0), 0), (piece_azf(1, 1), 0)], [])
+            step(index, True, dy, dz, summed_over_y() + [(piece_azf(1, 0), 0), (piece_azf(1, 1), 0)], [])
 
         @when(8)
         def _():
-            step(False, dy, dz, [], [
-                (piece_bzh(dy, 0), 0, z_peer[0]), (piece_bzh(dy, 1), HB[0], z_peer[1])])
+            step(index, False, dy, dz, [], first_of_b(dy))
 
         for d in (0, 1):
             @when(9 + d)
             def _(d=d):
-                step(False, dy, dz, [(piece_bzh(dy, d), d * HB[0])], [(piece_bzf(dy, 3, d), 0, z_peer[d])])
+                step(index, False, dy, dz, [(piece_bzh(dy, d), d * HB[0])], [(piece_bzf(dy, 3, d), 0, z_peer[d])])
 
         @when(11)
         def _():
-            step(False, dy, dz, [(piece_bzf(dy, hops + 1, toward), 0)],
+            step(index, False, dy, dz, [(piece_bzf(dy, hops + 1, toward), 0)],
                  [(piece_bzf(dy, hops, toward), 0, z_toward(toward))])
 
         def summed_over_z():
@@ -261,17 +288,45 @@
 
         @when(12)
         def _():
-            step(False, dy, dz, summed_over_z(), [
+            step(index, False, dy, dz, summed_over_z(), [
                 (piece_byh(0), 0, y_peer[0]), (piece_byh(1), HB[0], y_peer[1])])
 
         for d in (0, 1):
             @when(13 + d)
             def _(d=d):
-                step(False, dy, dz, summed_over_z() + [(piece_byh(d), d * HB[0])], [(piece_byf(d), 0, y_peer[d])])
+                step(index, False, dy, dz, summed_over_z() + [(piece_byh(d), d * HB[0])], [(piece_byf(d), 0, y_peer[d])])
 
         @when(15)
         def _():
-            step(False, dy, dz, summed_over_z() + [(piece_byf(0), 0), (piece_byf(1), 0)], [])
+            step(index, False, dy, dz, summed_over_z() + [(piece_byf(0), 0), (piece_byf(1), 0)], [])
+
+        def dispatch(low, high):
+            if high - low == 1:
+                if low in kinds:
+                    kinds[low]()
+                return
+            middle = (low + high) // 2
+            pl.when(kind < middle)(lambda: dispatch(low, middle))
+            pl.when(kind >= middle)(lambda: dispatch(middle, high))
+
+        dispatch(0, 16)
+
+    def sent(count, piece):
+        @pl.loop(0, count)
+        def _(index):
+            for copy in copies(piece(index), nowhere):
+                copy.wait_send()
+    def wait_for_sends():
+        for d in (0, 1):
+            sent(NZ, lambda i, d=d: piece_ayh(i, d))
+            sent(NZ, lambda i, d=d: piece_ayf(i, d))
+            sent(1, lambda i, d=d: piece_azh(d))
+            sent(3, lambda i, d=d: piece_azf(i + 1, d))
+            sent(NY, lambda i, d=d: piece_bzh(i, d))
+            for dy in range(NY):
+                sent(3, lambda i, d=d, dy=dy: piece_bzf(dy, i + 1, d))
+            sent(1, lambda i, d=d: piece_byh(d))
+            sent(1, lambda i, d=d: piece_byf(d))
 
     lanes = jnp.sum(sq_vec[0] + sq_vec[1], axis=0, keepdims=True)
     value = lanes[:, :128] + lanes[:, 128:256] + lanes[:, 256:]
@@ -288,41 +343,28 @@
             exchange.append(copy)
             place += 1
         if stage == 1:
+            wait_for_sends()
+        if stage == 2:
             grad_ref[...] = final[...].T
         for copy in exchange:
             copy.wait_recv()
         for slot in range(len(offsets)):
             value = value + slots[slot]
         waiting += exchange
-    sq_ref[...] = jnp.broadcast_to(jnp.sum(value, axis=1, keepdims=True), (8, 128))
+    threshold = clip_scale * math.sqrt(4 * NY * NZ * DB * UN * 2)
+    norm = jnp.sqrt(jnp.broadcast_to(jnp.sum(value, axis=1, keepdims=True), (1, UN)))
+    clip_ref[...] = jnp.minimum(1.0, threshold / norm)
 
     for copy in waiting:
         copy.wait_send()
-
-    def sent(count, piece):
-        @pl.loop(0, count)
-        def _(index):
-            for copy in copies(piece(index), nowhere):
-                copy.wait_send()
-
-    for d in (0, 1):
-        sent(NZ, lambda i, d=d: piece_ayh(i, d))
-        sent(NZ, lambda i, d=d: piece_ayf(i, d))
-        sent(1, lambda i, d=d: piece_azh(d))
-        sent(3, lambda i, d=d: piece_azf(i + 1, d))
-        sent(NY, lambda i, d=d: piece_bzh(i, d))
-        for dy in range(NY):
-            sent(3, lambda i, d=d, dy=dy: piece_bzf(dy, i + 1, d))
-        sent(1, lambda i, d=d: piece_byh(d))
-        sent(1, lambda i, d=d: piece_byf(d))
 
 
 def reduced_gradient(activations, cotangent):
     dma = pltpu.SemaphoreType.DMA
     return pl.pallas_call(
         kernel,
-        out_shape=(jax.ShapeDtypeStruct((DB, UN), f32), jax.ShapeDtypeStruct((8, 128), f32)),
-        in_specs=[pl.BlockSpec(memory_space=pl.ANY), pl.BlockSpec(memory_space=pltpu.VMEM)],
+        out_shape=(jax.ShapeDtypeStruct((DB, UN), f32), jax.ShapeDtypeStruct((1, UN), f32)),
+        in_specs=[pl.BlockSpec(memory_space=pl.ANY), pl.BlockSpec(memory_space=pltpu.HBM)],
         out_specs=[pl.BlockSpec(memory_space=pltpu.VMEM)] * 2,
         scratch_shapes=[
             pltpu.VMEM((TOK, NY * NZ * DB), jnp.bfloat16),
@@ -345,29 +387,56 @@
             dma((N_PIECES,)),
             dma((23,)),
             dma((23,)),
+            pltpu.VMEM((TOK, UN), jnp.bfloat16),
+            dma(()),
         ],
-        compiler_params=pltpu.CompilerParams(collective_id=0, has_side_effects=True, vmem_limit_bytes=56 << 20),
+        compiler_params=pltpu.CompilerParams(collective_id=0, has_side_effects=True, vmem_limit_bytes=46 << 20),
     )(activations, cotangent)
 
 
+def update_kernel(grad_ref, clip_ref, count_ref, params_ref, first_ref, second_ref, new_params_ref, new_first_ref, new_second_ref):
+    clip_factor = clip_ref[...]
+    steps_now = jnp.full((1, UN), count_ref[0], jnp.int32)
+
+    def power(base):
+        result, base = jnp.ones((1, UN), f32), jnp.full((1, UN), base, f32)
+        for bit in range(8):
+            result = jnp.where((steps_now >> bit) & 1 == 1, result * base, result)
+            base = base * base
+        return result
+
+    first_scale = learn_rate / (1.0 - power(beta_one))
+    second_scale = 1.0 / (1.0 - power(beta_two))
+    for row in range(0, UPDATE_ROWS, 8):
+        rows = pl.ds(row, 8)
+        clipped = clip_factor * grad_ref[rows]
+        new_first = beta_one * first_ref[0, rows] + (1.0 - beta_one) * clipped
+        new_second = beta_two * second_ref[0, rows] + (1.0 - beta_two) * clipped * clipped
+        change = first_scale * new_first / (jnp.sqrt(new_second * second_scale) + epsilon)
+        new_first_ref[0, rows] = new_first
+        new_second_ref[0, rows] = new_second
+        new_params_ref[0, rows] = params_ref[0, rows] * (1.0 - learn_rate * decay_rate) - change
+
+
+UPDATE_ROWS = 192
+
+
+def update(grad_shard, clip_factor, step_counts, params, first_moment, second_moment):
+    block = pl.BlockSpec((1, UPDATE_ROWS, UN), lambda i: (0, i, 0))
+    return pl.pallas_call(
+        update_kernel,
+        grid=(DB // UPDATE_ROWS,),
+        out_shape=(jax.ShapeDtypeStruct((1, DB, UN), f32),) * 3,
+        in_specs=[pl.BlockSpec((UPDATE_ROWS, UN), lambda i: (i, 0)), pl.BlockSpec((1, UN), lambda i: (0, 0)),
+                  pl.BlockSpec(memory_space=pltpu.SMEM), block, block, block],
+        out_specs=[block] * 3,
+        compiler_params=pltpu.CompilerParams(vmem_limit_bytes=16 << 20),
+    )(grad_shard, clip_factor, step_counts, params, first_moment, second_moment)
+
+
 def body(activations, cotangent, params, first_moment, second_moment, step_counts):
-    feature_count = activations.shape[2]
-    unit_count = cotangent.shape[2]
-    grad_shard, squares = reduced_gradient(activations, cotangent)
-    global_sq = squares[0, 0]
-    threshold = clip_scale * math.sqrt(
-        lax.axis_size("section") * feature_count * unit_count * lax.axis_size("tensor")
-    )
-    clip_factor = jnp.minimum(1.0, threshold / jnp.sqrt(global_sq))
-    clipped = clip_factor * grad_shard[None]
-    new_first = beta_one * first_moment + (1.0 - beta_one) * clipped
-    new_second = beta_two * second_moment + (1.0 - beta_two) * clipped * clipped
-    steps_now = step_counts[0].astype(jnp.float32)
-    first_fix = 1.0 - jnp.power(jnp.float32(beta_one), steps_now)
-    second_fix = 1.0 - jnp.power(jnp.float32(beta_two), steps_now)
-    update = new_first / first_fix / (jnp.sqrt(new_second / second_fix) + epsilon)
-    new_params = params * (1.0 - learn_rate * decay_rate) - learn_rate * update
-    return (new_params, new_first, new_second)
+    grad_shard, clip_factor = reduced_gradient(activations, pltpu.with_memory_space_constraint(cotangent, pltpu.HBM))
+    return update(grad_shard, clip_factor, step_counts, params, first_moment, second_moment)
 
 
 def solution(mesh):

time: 101 us -> 95.1 us (0.942)
  other arithmetic: 2.93 us -> 0 us
  local copies, waits for them, and re-layouts: 1.21 us -> 0.01 us
  Pallas kernels: 94.6 us -> 93.5 us
    sub x1 -> x0, other arithmetic: 2.93 us -> none  [body(): new_params = params * (1.0 - learn_rate * decay_rate) - learn_rate * update]
    pallas_call x1, Pallas kernels: 94.6 us -> 91.9 us  [reduced_gradient(): pl.pallas_call(kernel, out_shape=(jax.ShapeDtypeStruct((DB, UN), f32), ja...]
    pallas_call x0 -> x1, Pallas kernels: none -> 1.63 us  [update(): pl.pallas_call(update_kernel, grid=(DB // UPDATE_ROWS,), out_shape=(jax.S...]
    slice x1 -> x0, local copies, waits for them, and re-layouts: 1.19 us -> none  [body(): global_sq = squares[0, 0]]
where the time goes in v2:
time: 95.1 us; the launch traced here: 95 us
  Pallas kernels  93.5 us (98%)
  between operations  1.48 us (2%)
    pallas_call x1, Pallas kernels, reduced_gradient(): pl.pallas_call(kernel, out_shape=(jax.ShapeDtypeStruct((DB, UN), f32), ja...  91.9 us

profile of v2, /device:TPU:1, one launch (start us, length us, event | category | flops | bytes accessed | tf_op | source)
XLA Modules:
  0.0 95.0 jit_solution(4918382858227297035)
XLA Ops:
  0.6 0.0 copy-start.2
  0.6 0.0 copy-start.1
  0.7 0.0 copy-start
  1.5 91.9 %shard_map.85 = (f32[384,512]{1,0:T(8,128)S(1)}, f32[1,512]{1,0:T(1,128)S(1)}) custom-call(bf16[1,512,12288]{2,1,0:T(8,128)(2,1)} %act_ref.1, bf16[1,512,512]{2,1,0:T(8,128)(2,1)} %cot_hbm.1), custom_call_target="tpu_custom_call" | custom-call | tf_op jit(solution)/shard_map/pallas_call | solution.py:364
  93.4 0.0 copy-done.2
  93.4 0.0 copy-done.1
  93.4 0.0 copy-done
  93.4 1.6 %shard_map.86 = (f32[1,384,512]{2,1,0:T(8,128)}, f32[1,384,512]{2,1,0:T(8,128)}, f32[1,384,512]{2,1,0:T(8,128)}) custom-call(f32[384,512]{1,0:T(8,128)S(1)} %get-tuple-element.5.grad_ref, f32[1,512]{1,0:T(1,128)S(1)} %get-tuple-element.6.clip_ref, s32[1]{0:T(128)S(6)} %copy.9.count_ref, f32[1,384,512]{2,1,0:T(8,128)S(1)} %copy-done, ...), custom_call_target="tpu_custom_call" | custom-call | tf_op jit(solution)/shard_map/pallas_call | solution.py:426
Async XLA Ops:
  0.6 92.8 %copy-start.2 = (f32[1,384,512]{2,1,0:T(8,128)S(1)}, f32[1,384,512]{2,1,0:T(8,128)}, u32[]{:S(2)}) copy-start(f32[1,384,512]{2,1,0:T(8,128)} %second_ref.1) | copy-start | bytes 2359300
  0.6 92.8 %copy-start.1 = (f32[1,384,512]{2,1,0:T(8,128)S(1)}, f32[1,384,512]{2,1,0:T(8,128)}, u32[]{:S(2)}) copy-start(f32[1,384,512]{2,1,0:T(8,128)} %first_ref.1) | copy-start | bytes 2359300
  0.7 92.8 %copy-start = (f32[1,384,512]{2,1,0:T(8,128)S(1)}, f32[1,384,512]{2,1,0:T(8,128)}, u32[]{:S(2)}) copy-start(f32[1,384,512]{2,1,0:T(8,128)} %params_ref.1) | copy-start | bytes 2359300

commit v3 on v2

--- a/solution.py
+++ b/solution.py
@@ -21,6 +21,7 @@
 NY, NZ, DB, UN, TOK = 4, 8, 384, 512, 512
 RA, RB = 304, 208
 HA, HB = (160, 144), (96, 112)
+HA_Z, HB_Y = (176, 128), (32, 176)
 TILE = 16
 LEVELS = 32766.0
 
@@ -45,7 +46,7 @@
 
 
 def piece_azh(d):
-    return 32 + d, O_AZH + d * HA[0], HA[d]
+    return 32 + d, O_AZH + d * HA_Z[0], HA_Z[d]
 
 
 def piece_azf(j, d):
@@ -61,14 +62,14 @@
 
 
 def piece_byh(d):
-    return 72 + d, O_BYH + d * HB[0], HB[d]
+    return 72 + d, O_BYH + d * HB_Y[0], HB_Y[d]
 
 
 def piece_byf(d):
     return 74 + d, O_BYF + d * RB, RB
 
 
-SCHEDULE = [20, 268, 19, 276, 260, 18, 284, 22, 299, 333, 21, 291, 341, 44, 92, 307, 349, 23, 315, 93, 366, 45, 362, 374, 43, 100, 91, 354, 378, 325, 17, 367, 94, 46, 370, 165, 42, 131, 90, 47, 375, 377, 95, 369, 382, 16, 89, 198, 194, 358, 41, 383, 361, 400, 353, 88, 40, 199, 193, 424, 359, 472, 224, 480]
+SCHEDULE = [21, 276, 20, 268, 260, 19, 284, 18, 307, 341, 333, 44, 92, 299, 291, 325, 17, 349, 22, 43, 370, 91, 374, 315, 100, 45, 362, 93, 366, 23, 369, 358, 375, 46, 94, 131, 378, 42, 165, 90, 16, 367, 95, 354, 89, 47, 382, 361, 400, 194, 198, 41, 377, 383, 353, 359, 88, 424, 40, 199, 193, 472, 480, 224]
 
 
 def firsts(schedule):
@@ -250,12 +251,12 @@
         @when(3)
         def _():
             step(index, True, dy, dz, summed_over_y(), [
-                (piece_azh(0), 0, z_peer[0]), (piece_azh(1), HA[0], z_peer[1])])
+                (piece_azh(0), 0, z_peer[0]), (piece_azh(1), HA_Z[0], z_peer[1])])
 
         for d in (0, 1):
             @when(4 + d)
             def _(d=d):
-                step(index, True, dy, dz, summed_over_y() + [(piece_azh(d), d * HA[0])], [(piece_azf(3, d), 0, z_peer[d])])
+                step(index, True, dy, dz, summed_over_y() + [(piece_azh(d), d * HA_Z[0])], [(piece_azf(3, d), 0, z_peer[d])])
 
         toward = (dz > NZ // 2).astype(jnp.int32)
         hops = jnp.where(dz > NZ // 2, NZ - dz, dz)
@@ -289,12 +290,12 @@
         @when(12)
         def _():
             step(index, False, dy, dz, summed_over_z(), [
-                (piece_byh(0), 0, y_peer[0]), (piece_byh(1), HB[0], y_peer[1])])
+                (piece_byh(0), 0, y_peer[0]), (piece_byh(1), HB_Y[0], y_peer[1])])
 
         for d in (0, 1):
             @when(13 + d)
             def _(d=d):
-                step(index, False, dy, dz, summed_over_z() + [(piece_byh(d), d * HB[0])], [(piece_byf(d), 0, y_peer[d])])
+                step(index, False, dy, dz, summed_over_z() + [(piece_byh(d), d * HB_Y[0])], [(piece_byf(d), 0, y_peer[d])])
 
         @when(15)
         def _():

time: 95.1 us -> 94.8 us (level)
  no operation moved by 1% of the time
where the time goes in v3:
time: 94.8 us; the launch traced here: 94.7 us
  Pallas kernels  93.2 us (98%)
  between operations  1.48 us (2%)
    pallas_call x1, Pallas kernels, reduced_gradient(): pl.pallas_call(kernel, out_shape=(jax.ShapeDtypeStruct((DB, UN), f32), ja...  91.6 us

profile of v3, /device:TPU:1, one launch (start us, length us, event | category | flops | bytes accessed | tf_op | source)
XLA Modules:
  0.0 94.7 jit_solution(3994898399046123839)
XLA Ops:
  0.6 0.0 copy-start.2
  0.6 0.0 copy-start.1
  0.7 0.0 copy-start
  1.5 91.6 %shard_map.85 = (f32[384,512]{1,0:T(8,128)S(1)}, f32[1,512]{1,0:T(1,128)S(1)}) custom-call(bf16[1,512,12288]{2,1,0:T(8,128)(2,1)} %act_ref.1, bf16[1,512,512]{2,1,0:T(8,128)(2,1)} %cot_hbm.1), custom_call_target="tpu_custom_call" | custom-call | tf_op jit(solution)/shard_map/pallas_call | solution.py:365
  93.0 0.0 copy-done.2
  93.1 0.0 copy-done.1
  93.1 0.0 copy-done
  93.1 1.6 %shard_map.86 = (f32[1,384,512]{2,1,0:T(8,128)}, f32[1,384,512]{2,1,0:T(8,128)}, f32[1,384,512]{2,1,0:T(8,128)}) custom-call(f32[384,512]{1,0:T(8,128)S(1)} %get-tuple-element.5.grad_ref, f32[1,512]{1,0:T(1,128)S(1)} %get-tuple-element.6.clip_ref, s32[1]{0:T(128)S(6)} %copy.9.count_ref, f32[1,384,512]{2,1,0:T(8,128)S(1)} %copy-done, ...), custom_call_target="tpu_custom_call" | custom-call | tf_op jit(solution)/shard_map/pallas_call | solution.py:427
Async XLA Ops:
  0.6 92.4 %copy-start.2 = (f32[1,384,512]{2,1,0:T(8,128)S(1)}, f32[1,384,512]{2,1,0:T(8,128)}, u32[]{:S(2)}) copy-start(f32[1,384,512]{2,1,0:T(8,128)} %second_ref.1) | copy-start | bytes 2359300
  0.6 92.4 %copy-start.1 = (f32[1,384,512]{2,1,0:T(8,128)S(1)}, f32[1,384,512]{2,1,0:T(8,128)}, u32[]{:S(2)}) copy-start(f32[1,384,512]{2,1,0:T(8,128)} %first_ref.1) | copy-start | bytes 2359300
  0.7 92.4 %copy-start = (f32[1,384,512]{2,1,0:T(8,128)S(1)}, f32[1,384,512]{2,1,0:T(8,128)}, u32[]{:S(2)}) copy-start(f32[1,384,512]{2,1,0:T(8,128)} %params_ref.1) | copy-start | bytes 2359300

commit v4 on v3

--- a/solution.py
+++ b/solution.py
@@ -98,9 +98,13 @@
 EARLY = 2
 
 
+def farthest_first(offsets):
+    return sorted(offsets, key=lambda o: -(min(o[0], 4 - o[0]) + min(o[1], NY - o[1]) + min(o[2], NZ - o[2])))
+
+
 PEERS_C = [(0, 0, 0, 1)]
-PEERS_XY = [(i, j, 0, 0) for i in range(4) for j in range(4) if i or j]
-PEERS_Z = [(0, 0, i, 0) for i in range(1, 8)]
+PEERS_XY = farthest_first([(i, j, 0, 0) for i in range(4) for j in range(4) if i or j])
+PEERS_Z = farthest_first([(0, 0, i, 0) for i in range(1, 8)])
 
 
 def kernel(act_ref, cot_hbm, grad_ref, clip_ref, act, cot_t, total, final, send, recv, send_scale, recv_scale,
@@ -123,7 +127,7 @@
         return pl.ds(pl.multiple_of(block * DB, DB), DB)
 
     barrier = pltpu.get_barrier_semaphore()
-    peers = PEERS_C + PEERS_XY + PEERS_Z
+    peers = farthest_first(PEERS_C + PEERS_XY + PEERS_Z)
     for offset in peers:
         pl.semaphore_signal(barrier, inc=1, device_id=peer(*offset), device_id_type=MESH)
 

time: 94.8 us -> 94.8 us (level)
  no operation moved by 1% of the time
where the time goes in v4:
time: 94.8 us; the launch traced here: 94.7 us
  Pallas kernels  93.2 us (98%)
  between operations  1.48 us (2%)
    pallas_call x1, Pallas kernels, reduced_gradient(): pl.pallas_call(kernel, out_shape=(jax.ShapeDtypeStruct((DB, UN), f32), ja...  91.6 us

profile of v4, /device:TPU:1, one launch (start us, length us, event | category | flops | bytes accessed | tf_op | source)
XLA Modules:
  0.0 94.7 jit_solution(15618458911321598920)
XLA Ops:
  0.6 0.0 copy-start.2
  0.6 0.0 copy-start.1
  0.7 0.0 copy-start
  1.5 91.6 %shard_map.85 = (f32[384,512]{1,0:T(8,128)S(1)}, f32[1,512]{1,0:T(1,128)S(1)}) custom-call(bf16[1,512,12288]{2,1,0:T(8,128)(2,1)} %act_ref.1, bf16[1,512,512]{2,1,0:T(8,128)(2,1)} %cot_hbm.1), custom_call_target="tpu_custom_call" | custom-call | tf_op jit(solution)/shard_map/pallas_call | solution.py:369
  93.1 0.0 copy-done.2
  93.1 0.0 copy-done.1
  93.1 0.0 copy-done
  93.1 1.6 %shard_map.86 = (f32[1,384,512]{2,1,0:T(8,128)}, f32[1,384,512]{2,1,0:T(8,128)}, f32[1,384,512]{2,1,0:T(8,128)}) custom-call(f32[384,512]{1,0:T(8,128)S(1)} %get-tuple-element.5.grad_ref, f32[1,512]{1,0:T(1,128)S(1)} %get-tuple-element.6.clip_ref, s32[1]{0:T(128)S(6)} %copy.9.count_ref, f32[1,384,512]{2,1,0:T(8,128)S(1)} %copy-done, ...), custom_call_target="tpu_custom_call" | custom-call | tf_op jit(solution)/shard_map/pallas_call | solution.py:431
Async XLA Ops:
  0.6 92.4 %copy-start.2 = (f32[1,384,512]{2,1,0:T(8,128)S(1)}, f32[1,384,512]{2,1,0:T(8,128)}, u32[]{:S(2)}) copy-start(f32[1,384,512]{2,1,0:T(8,128)} %second_ref.1) | copy-start | bytes 2359300
  0.6 92.4 %copy-start.1 = (f32[1,384,512]{2,1,0:T(8,128)S(1)}, f32[1,384,512]{2,1,0:T(8,128)}, u32[]{:S(2)}) copy-start(f32[1,384,512]{2,1,0:T(8,128)} %first_ref.1) | copy-start | bytes 2359300
  0.7 92.4 %copy-start = (f32[1,384,512]{2,1,0:T(8,128)S(1)}, f32[1,384,512]{2,1,0:T(8,128)}, u32[]{:S(2)}) copy-start(f32[1,384,512]{2,1,0:T(8,128)} %params_ref.1) | copy-start | bytes 2359300

commit v5 on v4

--- a/solution.py
+++ b/solution.py
@@ -95,7 +95,7 @@
     return values[0]
 
 
-EARLY = 2
+EARLY = 3
 
 
 def farthest_first(offsets):

time: 94.8 us -> 95.3 us (level)
  no operation moved by 1% of the time
where the time goes in v5:
time: 95.3 us; the launch traced here: 95.2 us
  Pallas kernels  93.8 us (98%)
  between operations  1.48 us (2%)
    pallas_call x1, Pallas kernels, reduced_gradient(): pl.pallas_call(kernel, out_shape=(jax.ShapeDtypeStruct((DB, UN), f32), ja...  92.1 us

profile of v5, /device:TPU:1, one launch (start us, length us, event | category | flops | bytes accessed | tf_op | source)
XLA Modules:
  0.0 95.2 jit_solution(248773361459737982)
XLA Ops:
  0.6 0.0 copy-start.2
  0.6 0.0 copy-start.1
  0.7 0.0 copy-start
  1.5 92.1 %shard_map.85 = (f32[384,512]{1,0:T(8,128)S(1)}, f32[1,512]{1,0:T(1,128)S(1)}) custom-call(bf16[1,512,12288]{2,1,0:T(8,128)(2,1)} %act_ref.1, bf16[1,512,512]{2,1,0:T(8,128)(2,1)} %cot_hbm.1), custom_call_target="tpu_custom_call" | custom-call | tf_op jit(solution)/shard_map/pallas_call | solution.py:369
  93.6 0.0 copy-done.2
  93.6 0.0 copy-done.1
  93.6 0.0 copy-done
  93.6 1.6 %shard_map.86 = (f32[1,384,512]{2,1,0:T(8,128)}, f32[1,384,512]{2,1,0:T(8,128)}, f32[1,384,512]{2,1,0:T(8,128)}) custom-call(f32[384,512]{1,0:T(8,128)S(1)} %get-tuple-element.5.grad_ref, f32[1,512]{1,0:T(1,128)S(1)} %get-tuple-element.6.clip_ref, s32[1]{0:T(128)S(6)} %copy.9.count_ref, f32[1,384,512]{2,1,0:T(8,128)S(1)} %copy-done, ...), custom_call_target="tpu_custom_call" | custom-call | tf_op jit(solution)/shard_map/pallas_call | solution.py:431
Async XLA Ops:
  0.6 93.0 %copy-start.2 = (f32[1,384,512]{2,1,0:T(8,128)S(1)}, f32[1,384,512]{2,1,0:T(8,128)}, u32[]{:S(2)}) copy-start(f32[1,384,512]{2,1,0:T(8,128)} %second_ref.1) | copy-start | bytes 2359300
  0.6 93.0 %copy-start.1 = (f32[1,384,512]{2,1,0:T(8,128)S(1)}, f32[1,384,512]{2,1,0:T(8,128)}, u32[]{:S(2)}) copy-start(f32[1,384,512]{2,1,0:T(8,128)} %first_ref.1) | copy-start | bytes 2359300
  0.7 93.0 %copy-start = (f32[1,384,512]{2,1,0:T(8,128)S(1)}, f32[1,384,512]{2,1,0:T(8,128)}, u32[]{:S(2)}) copy-start(f32[1,384,512]{2,1,0:T(8,128)} %params_ref.1) | copy-start | bytes 2359300
